TPU v7x, 32 devices: a whole 2x2x4 slice. The times are simulated.
32 devices in a mesh: slab: 8 (over z, x), pencil: 4 (over y, core).
Axes of the slice: x: 2, y: 2, z: 4, core: 2. Of those that a mesh axis runs over, the one named last changes fastest.
Arguments:
- basis: bfloat16 [88, 64, 128, 128], P(None, 'slab', 'pencil'), may hold values from -6 to 6
- image: bfloat16 [88, 64, 128, 128], P(None, 'slab', 'pencil'), may hold values from -6.3 to 6.3
- material: int32 [64, 128, 128], P('slab', 'pencil'), may hold values from 0 to 3
- picked: int32 [32], replicated, may hold values from 0 to 87, as said below
Outputs:
- recycle_out: float32 [32, 64, 128, 128], P(None, 'slab', 'pencil')
- images_out: float32 [32, 64, 128, 128], P(None, 'slab', 'pencil')
Inputs may be any that keep to these rules, and one draw needn't show every extreme that they name: `picked`: 32 distinct column numbers.
All inputs are finite; a program needn't handle non-finite values.
Results may differ from a plain program's by a relative error of at most 0.0061.
Values may be sent and summed in bfloat16 or wider, within the bound.
A program may use at most 128 MiB of HBM per device.

v0:
```python
import functools

import jax
import jax.numpy as jnp
from jax import lax
from jax.experimental import pallas as pl
from jax.experimental.pallas import tpu as pltpu
from jax.sharding import PartitionSpec as P

MESH = pl.DeviceIdType.MESH
F32 = jnp.float32
BF16 = jnp.bfloat16
GROUP = 8
PITCH = 40
LANES = 128


def dot_nt(a, b):
    return lax.dot_general(a, b, (((1,), (1,)), ((), ())), preferred_element_type=F32)


def split(value):
    high = value.astype(BF16)
    return high, (value - high.astype(F32)).astype(BF16)


def splat(tile, column):
    return jnp.broadcast_to(tile[:, column:column + 1], tile.shape)


def row_of(tile, index):
    return jnp.broadcast_to(tile[index:index + 1, :], tile.shape)


def merge_rows(tile, rows, first):
    index = lax.broadcasted_iota(jnp.int32, tile.shape, 0)
    for offset, row in enumerate(rows):
        tile = jnp.where(index == first + offset, row, tile)
    return tile


def pivot_block(tiles, step):
    block, first = step // 2, 4 * (step % 2)
    columns = [[splat(tile, 4 * step + j) for j in range(4)] for tile in tiles]
    rows = [row_of(tiles[block], first + i) for i in range(4)]
    pivots = [[row_of(columns[block][j], first + i) for j in range(4)] for i in range(4)]
    return block, first, columns, rows, pivots


def solve_spd(tiles, unknowns):
    for step in range(unknowns // 4):
        block, first, columns, rows, pivots = pivot_block(tiles, step)
        for j in range(4):
            scale = 1.0 / pivots[j][j]
            rows[j] = rows[j] * scale
            for c in range(j + 1, 4):
                pivots[j][c] = pivots[j][c] * scale
            for i in range(4):
                if i != j:
                    factor = pivots[i][j]
                    rows[i] = rows[i] - factor * rows[j]
                    for c in range(j + 1, 4):
                        pivots[i][c] = pivots[i][c] - factor * pivots[j][c]
        updated = []
        for t, tile in enumerate(tiles):
            for j in range(4):
                tile = tile - columns[t][j] * rows[j]
            if t == block:
                tile = merge_rows(tile, rows, first)
            updated.append(tile)
        tiles = updated
    return tiles


def eliminate(tiles, unknowns):
    for step in range(unknowns // 4):
        block, first, columns, rows, pivots = pivot_block(tiles, step)
        done = []
        for j in range(4):
            scale = 1.0 / pivots[j][j]
            done.append(rows[j] * lax.rsqrt(pivots[j][j]))
            rows[j] = rows[j] * scale
            for c in range(j + 1, 4):
                pivots[j][c] = pivots[j][c] * scale
            for i in range(4):
                if i != j:
                    factor = pivots[i][j]
                    rows[i] = rows[i] - factor * rows[j]
                    for c in range(j + 1, 4):
                        pivots[i][c] = pivots[i][c] - factor * pivots[j][c]
        index = lax.broadcasted_iota(jnp.int32, tiles[0].shape, 0)
        updated = []
        for t, tile in enumerate(tiles):
            if t < block:
                updated.append(tile)
                continue
            changed = tile
            for j in range(4):
                changed = changed - columns[t][j] * rows[j]
            if t == block:
                changed = jnp.where(index >= first + 4, changed, tile)
                changed = merge_rows(changed, done, first)
            updated.append(changed)
        tiles = updated
    return tiles


def all_sum(part, slots, gathered, total, sems, slabs, pencils):
    slab, pencil = lax.axis_index("slab"), lax.axis_index("pencil")
    scatter_send, scatter_recv, slab_send, slab_recv, back_send, back_recv = sems
    rows = part.shape[0] // pencils

    def chunk(index):
        return pl.ds(pl.multiple_of(index * rows, rows), rows)

    copies = []
    for d in range(1, pencils):
        peer = lax.rem(pencil + d, pencils)
        copies.append(pltpu.make_async_remote_copy(
            src_ref=part.at[chunk(peer)], dst_ref=slots.at[d - 1],
            send_sem=scatter_send.at[d - 1], recv_sem=scatter_recv.at[d - 1],
            device_id={"slab": slab, "pencil": peer}, device_id_type=MESH))
    for copy in copies:
        copy.start()
    mine = part[chunk(pencil), :]
    for d, copy in enumerate(copies):
        copy.wait_recv()
        mine = mine + slots[d]
    gathered[slab] = mine
    slab_copies = []
    for d in range(1, slabs):
        peer = lax.rem(slab + d, slabs)
        slab_copies.append(pltpu.make_async_remote_copy(
            src_ref=gathered.at[slab], dst_ref=gathered.at[slab],
            send_sem=slab_send.at[d - 1], recv_sem=slab_recv.at[d - 1],
            device_id={"slab": peer, "pencil": pencil}, device_id_type=MESH))
    for copy in slab_copies:
        copy.start()
    for copy in slab_copies:
        copy.wait_recv()
    summed = gathered[0]
    for s in range(1, slabs):
        summed = summed + gathered[s]
    total[chunk(pencil), :] = summed
    back_copies = []
    for d in range(1, pencils):
        peer = lax.rem(pencil + d, pencils)
        back_copies.append(pltpu.make_async_remote_copy(
            src_ref=total.at[chunk(pencil)], dst_ref=total.at[chunk(pencil)],
            send_sem=back_send.at[d - 1], recv_sem=back_recv.at[d - 1],
            device_id={"slab": slab, "pencil": peer}, device_id_type=MESH))
    for copy in back_copies:
        copy.start()
    for copy in back_copies:
        copy.wait_recv()
    for copy in copies + slab_copies + back_copies:
        copy.wait_send()


def main_kernel(
    slabs, pencils, count, cells,
    basis_ref, image_ref, material_ref, picked_ref,
    rec_out, app_out, inverse_out,
    basis_in, image_in, wide, rows_of_basis, weights, rec, app, factor,
    z_send, z_halo, y_send, y_halo,
    part1, slots1, gathered1, total1, part2, slots2, gathered2, total2, turned,
    in_sems, out_sems, halo_send, halo_recv, *sum_sems,
):
    columns, depth, height, width = basis_in.shape[1], *basis_in.shape[:1], *basis_in.shape[2:]
    groups = height // GROUP
    slab, pencil = lax.axis_index("slab"), lax.axis_index("pencil")

    loads = []
    for z in range(depth):
        for which, (source, target) in enumerate(((basis_ref, basis_in), (image_ref, image_in))):
            loads.append(pltpu.make_async_copy(
                source.at[:, z], target.at[z], in_sems.at[2 * z + which]))
    for load in loads:
        load.start()

    barrier = pltpu.get_barrier_semaphore()
    for d in range(1, pencils):
        pl.semaphore_signal(
            barrier, inc=1, device_id={"slab": slab, "pencil": lax.rem(pencil + d, pencils)},
            device_id_type=MESH)
    for d in range(1, slabs):
        pl.semaphore_signal(
            barrier, inc=1, device_id={"slab": lax.rem(slab + d, slabs), "pencil": pencil},
            device_id_type=MESH)

    material = material_ref[...]
    factor[...] = 6.0 - jnp.where(
        material == 0, 0.3,
        jnp.where(material == 1, 0.9, jnp.where(material == 2, 1.6, 2.5))).astype(F32)

    extra = 16 - columns % 16 if columns % 16 else 0
    low = columns - extra
    flat = wide.reshape(2 * columns * PITCH, width)
    gram = jnp.zeros((columns + extra, 2 * columns), F32)
    for z in range(depth):
        loads[2 * z].wait()
        wide[0:columns, 0:height, :] = basis_in[z].astype(F32)
        loads[2 * z + 1].wait()
        wide[columns:2 * columns, 0:height, :] = image_in[z].astype(F32)
        for g in range(groups):
            turned_rows = []
            for y in range(g * GROUP, (g + 1) * GROUP):
                both = flat[pl.ds(y, 2 * columns, stride=PITCH), :].astype(BF16)
                rows_of_basis[z, y] = both[0:columns + extra]
                turned_rows.append(both)
            stacked = jnp.concatenate(turned_rows, axis=1)
            gram = gram + dot_nt(stacked[low:], stacked)

    source_row = lax.broadcasted_iota(jnp.int32, (2 * columns, LANES), 0)
    lane = lax.broadcasted_iota(jnp.int32, (2 * columns, LANES), 1)
    wanted = jnp.where(
        lane < columns, lane + columns, jnp.broadcast_to(picked_ref[...], (2 * columns, LANES)))
    select = jnp.where(source_row == wanted, 1.0, 0.0).astype(BF16)
    high, rest = gram.astype(BF16), gram
    augmented = jnp.dot(high, select, preferred_element_type=F32)
    for _ in range(2):
        rest = rest - high.astype(F32)
        high = rest.astype(BF16)
        augmented = augmented + jnp.dot(high, select, preferred_element_type=F32)
    part1[...] = augmented

    pl.semaphore_wait(barrier, slabs + pencils - 2)
    all_sum(part1, slots1, gathered1, total1, sum_sems[0:6], slabs, pencils)

    tiles = [total1[extra + 8 * t:extra + 8 * (t + 1), :] for t in range(columns // 8)]
    tiles = solve_spd(tiles, columns)
    turned[...] = jnp.zeros_like(turned)
    for t, tile in enumerate(tiles):
        turned[8 * t:8 * (t + 1), :] = tile
    weights[...] = turned[...].T[columns:columns + count, 0:columns + extra].astype(BF16)

    def recycle_layer(z):
        for g in range(groups):
            cells_in = jnp.concatenate(
                [rows_of_basis[z, y] for y in range(g * GROUP, (g + 1) * GROUP)], axis=1)
            result = jnp.dot(weights[...], cells_in, preferred_element_type=F32)
            for i in range(GROUP):
                rec[z + 1, 1 + g * GROUP + i] = result[:, i * width:(i + 1) * width]

    def z_copy(side, peer):
        return pltpu.make_async_remote_copy(
            src_ref=z_send.at[side], dst_ref=z_halo.at[side],
            send_sem=halo_send.at[side], recv_sem=halo_recv.at[side],
            device_id={"slab": peer, "pencil": pencil}, device_id_type=MESH)

    def y_copy(side, peer):
        return pltpu.make_async_remote_copy(
            src_ref=y_send.at[side], dst_ref=y_halo.at[side],
            send_sem=halo_send.at[2 + side], recv_sem=halo_recv.at[2 + side],
            device_id={"slab": slab, "pencil": peer}, device_id_type=MESH)

    z_copies = (z_copy(0, lax.rem(slab + 1, slabs)), z_copy(1, lax.rem(slab + slabs - 1, slabs)))
    y_copies = (y_copy(0, lax.rem(pencil + 1, pencils)),
                y_copy(1, lax.rem(pencil + pencils - 1, pencils)))
    sends = (slab < slabs - 1, slab > 0, pencil < pencils - 1, pencil > 0)
    takes = (slab > 0, slab < slabs - 1, pencil > 0, pencil < pencils - 1)

    recycle_layer(depth - 1)
    z_send[0] = rec[depth, 1:height + 1].astype(BF16)
    pl.when(sends[0])(z_copies[0].start)
    recycle_layer(0)
    z_send[1] = rec[1, 1:height + 1].astype(BF16)
    pl.when(sends[1])(z_copies[1].start)
    pl.loop(1, depth - 1)(recycle_layer)
    y_send[0] = rec[1:depth + 1, height].astype(BF16)
    pl.when(sends[2])(y_copies[0].start)
    y_send[1] = rec[1:depth + 1, 1].astype(BF16)
    pl.when(sends[3])(y_copies[1].start)
    rec_store = pltpu.make_async_copy(
        rec.at[pl.ds(1, depth), pl.ds(1, height)], rec_out, out_sems.at[0])
    rec_store.start()

    lanes = lax.broadcasted_iota(jnp.int32, (count, width), 1)

    def applied_layer(z, normal):
        for g in range(groups):
            values = []
            for y in range(g * GROUP, (g + 1) * GROUP):
                center = rec[z + 1, y + 1]
                beside = rec[z, y + 1] + rec[z + 2, y + 1] + rec[z + 1, y] + rec[z + 1, y + 2]
                beside = beside + jnp.where(lanes == 0, 0.0, pltpu.roll(center, 1, 1))
                beside = beside + jnp.where(
                    lanes == width - 1, 0.0, pltpu.roll(center, width - 1, 1))
                value = factor[z, y:y + 1, :] * center - beside
                app[z, y] = value
                values.append(value)
            high, rest = split(jnp.concatenate(values, axis=1))
            both = jnp.concatenate([high, rest], axis=0)
            normal = normal + dot_nt(both, both)
        return normal

    for side, (take, send) in enumerate(zip(takes[2:], sends[2:])):
        pl.when(take)(y_copies[side].wait_recv)

        @pl.when(jnp.logical_not(take))
        def _():
            y_halo[side] = jnp.zeros(y_halo.shape[1:], BF16)

        rec[1:depth + 1, 0 if side == 0 else height + 1] = y_halo[side].astype(F32)
    normal = lax.fori_loop(1, depth - 1, applied_layer, jnp.zeros((2 * count, 2 * count), F32))
    for side, take in enumerate(takes[:2]):
        pl.when(take)(z_copies[side].wait_recv)

        @pl.when(jnp.logical_not(take))
        def _():
            z_halo[side] = jnp.zeros(z_halo.shape[1:], BF16)

        rec[0 if side == 0 else depth + 1, 1:height + 1] = z_halo[side].astype(F32)
        normal = applied_layer(0 if side == 0 else depth - 1, normal)
    app_store = pltpu.make_async_copy(app, app_out, out_sems.at[1])
    app_store.start()

    turned[0:2 * count, 0:2 * count] = normal
    halves = turned[0:count, :] + turned[count:2 * count, :]
    part2[...] = halves + pltpu.roll(halves, LANES - count, 1)
    all_sum(part2, slots2, gathered2, total2, sum_sems[6:12], slabs, pencils)

    row = lax.broadcasted_iota(jnp.int32, (count, LANES), 0)
    lane = lax.broadcasted_iota(jnp.int32, (count, LANES), 1)
    matrix = jnp.where(
        lane < count, total2[...] * (1.0 / cells), jnp.where(lane == row + count, 1.0, 0.0))
    tiles = eliminate([matrix[8 * t:8 * (t + 1), :] for t in range(count // 8)], count)
    inverse = pltpu.roll(jnp.concatenate(tiles, axis=0), LANES - count, 1)
    inverse = jnp.where(lane <= row, inverse, 0.0)
    high = inverse.astype(BF16).astype(F32)
    rest = (inverse - high).astype(BF16).astype(F32)
    inverse_out[...] = high + pltpu.roll(high, count, 1) + pltpu.roll(rest, 2 * count, 1)

    for copy, send in zip(z_copies + y_copies, sends):
        pl.when(send)(copy.wait_send)
    rec_store.wait()
    app_store.wait()


def final_kernel(inverse_ref, rec_ref, app_ref, rec_out, app_out):
    height, count, width = rec_ref.shape
    factors = inverse_ref[...][:, 0:3 * count].astype(BF16)
    for source, target in ((rec_ref, rec_out), (app_ref, app_out)):
        flat = target.reshape(count * height, width)
        for g in range(height // GROUP):
            values = jnp.concatenate(
                [source[y] for y in range(g * GROUP, (g + 1) * GROUP)], axis=1)
            high, rest = split(values)
            result = jnp.dot(
                factors, jnp.concatenate([high, rest, high], axis=0), preferred_element_type=F32)
            for i in range(GROUP):
                flat[pl.ds(g * GROUP + i, count, stride=height), :] = (
                    result[:, i * width:(i + 1) * width])


def local(slabs, pencils, basis, image, material, picked):
    columns, depth, height, width = basis.shape
    count = picked.shape[0]
    extra = 16 - columns % 16 if columns % 16 else 0
    padded = columns + extra
    cells = depth * height * width * slabs * pencils
    lanes = jnp.pad(
        picked[None, :], ((0, 0), (columns, LANES - columns - count)), constant_values=-1)

    def sum_scratch(rows):
        return [
            pltpu.VMEM((rows, LANES), F32),
            pltpu.VMEM((pencils - 1, rows // pencils, LANES), F32),
            pltpu.VMEM((slabs, rows // pencils, LANES), F32),
            pltpu.VMEM((rows, LANES), F32),
        ]

    def sum_sems():
        return [pltpu.SemaphoreType.DMA((n - 1,)) for n in (
            pencils, pencils, slabs, slabs, pencils, pencils)]

    in_vmem = pl.BlockSpec(memory_space=pltpu.VMEM)
    anywhere = pl.BlockSpec(memory_space=pl.ANY)
    turned_shape = jax.ShapeDtypeStruct((depth, height, count, width), F32)
    rec, app, inverse = pl.pallas_call(
        functools.partial(main_kernel, slabs, pencils, count, cells),
        out_shape=(turned_shape, turned_shape, jax.ShapeDtypeStruct((count, LANES), F32)),
        in_specs=[anywhere, anywhere, in_vmem, in_vmem],
        out_specs=(anywhere, anywhere, in_vmem),
        scratch_shapes=[
            pltpu.VMEM((depth, columns, height, width), BF16),
            pltpu.VMEM((depth, columns, height, width), BF16),
            pltpu.VMEM((2 * columns, PITCH, width), F32),
            pltpu.VMEM((depth, height, padded, width), BF16),
            pltpu.VMEM((count, padded), BF16),
            pltpu.VMEM((depth + 2, height + 2, count, width), F32),
            pltpu.VMEM((depth, height, count, width), F32),
            pltpu.VMEM((depth, height, width), F32),
            pltpu.VMEM((2, height, count, width), BF16),
            pltpu.VMEM((2, height, count, width), BF16),
            pltpu.VMEM((2, depth, count, width), BF16),
            pltpu.VMEM((2, depth, count, width), BF16),
            *sum_scratch(padded),
            *sum_scratch(count),
            pltpu.VMEM((LANES, LANES), F32),
            pltpu.SemaphoreType.DMA((2 * depth,)),
            pltpu.SemaphoreType.DMA((2,)),
            pltpu.SemaphoreType.DMA((4,)),
            pltpu.SemaphoreType.DMA((4,)),
            *sum_sems(),
            *sum_sems(),
        ],
        compiler_params=pltpu.CompilerParams(
            collective_id=0, has_side_effects=True, vmem_limit_bytes=56 * 1024 * 1024),
        name="recycle_update",
    )(basis, image, material, lanes)
    whole = pl.BlockSpec((None, height, count, width), lambda z: (z, 0, 0, 0))
    placed = pl.BlockSpec((count, None, height, width), lambda z: (0, z, 0, 0))
    out = jax.ShapeDtypeStruct((count, depth, height, width), F32)
    return pl.pallas_call(
        final_kernel,
        grid=(depth,),
        out_shape=(out, out),
        in_specs=[pl.BlockSpec((count, LANES), lambda z: (0, 0)), whole, whole],
        out_specs=(placed, placed),
        compiler_params=pltpu.CompilerParams(vmem_limit_bytes=32 * 1024 * 1024),
        name="times_inverse",
    )(inverse, rec, app)


def solution(mesh):
    placed = (
        P(None, "slab", "pencil", None),
        P(None, "slab", "pencil", None),
        P("slab", "pencil", None),
        P(),
    )
    return jax.shard_map(
        functools.partial(local, mesh.shape["slab"], mesh.shape["pencil"]),
        mesh=mesh,
        in_specs=placed,
        out_specs=(P(None, "slab", "pencil", None), P(None, "slab", "pencil", None)),
        check_vma=False,
    )
```

profile of v0, /device:TPU:0, one launch (start us, length us, event | category | flops | bytes accessed | tf_op | source)
XLA Modules:
  0.0 69.2 jit_solution(16847014008504121617)
XLA Ops:
  0.6 1.2 %pad.4.picked_ref = s32[1,128]{1,0:T(1,128)} pad(s32[1,32]{1,0:T(1,128)} %bitcast.1, s32[]{:T(128)} %constant.0.clone.1), padding=0_0x88_8 | pad | bytes 644 | tf_op jit(solution)/shard_map/jit(_pad)/pad | solution.py:362
  1.9 54.2 %recycle_update.1 = (f32[8,32,32,128]{3,2,1,0:T(8,128)}, f32[8,32,32,128]{3,2,1,0:T(8,128)}, f32[32,128]{1,0:T(8,128)}) custom-call(bf16[88,8,32,128]{3,2,1,0:T(8,128)(2,1)} %basis_ref.1, bf16[88,8,32,128]{3,2,1,0:T(8,128)(2,1)} %image_ref.1, s32[8,32,128]{2,1,0:T(8,128)} %material_ref.1, s32[1,128]{1,0:T(1,128)} %pad.4.picked_ref), custom_call_target="tpu_custom_call" | custom-call | tf_op jit(solution)/shard_map/recycle_update/pallas_call | solution.py:380
  56.1 0.0 copy-start
  56.1 2.2 %copy-done = f32[8,32,32,128]{3,2,1,0:T(8,128)S(1)} copy-done((f32[8,32,32,128]{3,2,1,0:T(8,128)S(1)}, f32[8,32,32,128]{3,2,1,0:T(8,128)}, u32[]{:S(2)}) %copy-start) | copy-done | bytes 4194328
  58.3 0.0 copy-start.1
  58.3 2.2 %copy-done.1 = f32[8,32,32,128]{3,2,1,0:T(8,128)S(1)} copy-done((f32[8,32,32,128]{3,2,1,0:T(8,128)S(1)}, f32[8,32,32,128]{3,2,1,0:T(8,128)}, u32[]{:S(2)}) %copy-start.1) | copy-done | bytes 4194328
  60.5 0.0 copy-start.2
  60.5 0.7 %copy-done.2 = f32[32,128]{1,0:T(8,128)S(1)} copy-done((f32[32,128]{1,0:T(8,128)S(1)}, f32[32,128]{1,0:T(8,128)}, u32[]{:S(2)}) %copy-start.2) | copy-done | bytes 16408
  61.2 8.0 %times_inverse.1 = (f32[32,8,32,128]{3,2,1,0:T(8,128)}, f32[32,8,32,128]{3,2,1,0:T(8,128)}) custom-call(f32[32,128]{1,0:T(8,128)S(1)} %copy-done.2, f32[8,32,32,128]{3,2,1,0:T(8,128)S(1)} %copy-done, f32[8,32,32,128]{3,2,1,0:T(8,128)S(1)} %copy-done.1), custom_call_target="tpu_custom_call" | custom-call | tf_op jit(solution)/shard_map/times_inverse/pallas_call | solution.py:415
Async XLA Ops:
  56.1 2.2 %copy-start = (f32[8,32,32,128]{3,2,1,0:T(8,128)S(1)}, f32[8,32,32,128]{3,2,1,0:T(8,128)}, u32[]{:S(2)}) copy-start(f32[8,32,32,128]{3,2,1,0:T(8,128)} %get-tuple-element.6.rec_ref) | copy-start | bytes 12582916
  58.3 2.2 %copy-start.1 = (f32[8,32,32,128]{3,2,1,0:T(8,128)S(1)}, f32[8,32,32,128]{3,2,1,0:T(8,128)}, u32[]{:S(2)}) copy-start(f32[8,32,32,128]{3,2,1,0:T(8,128)} %get-tuple-element.7.app_ref) | copy-start | bytes 12582916
  60.5 0.7 %copy-start.2 = (f32[32,128]{1,0:T(8,128)S(1)}, f32[32,128]{1,0:T(8,128)}, u32[]{:S(2)}) copy-start(f32[32,128]{1,0:T(8,128)} %get-tuple-element.5.inverse_ref) | copy-start | bytes 49156
where the time goes:
time: 69.5 us; the launch traced here: 69.2 us
  Pallas kernels  62.2 us (89%)
  local copies, waits for them, and re-layouts  6.32 us (9%)
    pallas_call x1, Pallas kernels, local(): pl.pallas_call(functools.partial(main_kernel, slabs, pencils, count, cell...  54.2 us
    pallas_call x1, Pallas kernels, local(): pl.pallas_call(final_kernel, grid=(depth,), out_shape=(out, out), in_spec...  8.01 us
    unnamed x6, local copies, waits for them, and re-layouts  5.09 us

commit v1 on v0

--- a/solution.py
+++ b/solution.py
@@ -11,7 +11,7 @@
 F32 = jnp.float32
 BF16 = jnp.bfloat16
 GROUP = 8
-PITCH = 40
+PITCH_EXTRA = 1
 LANES = 128
 
 
@@ -195,27 +195,37 @@
 
     extra = 16 - columns % 16 if columns % 16 else 0
     low = columns - extra
-    flat = wide.reshape(2 * columns * PITCH, width)
-    gram = jnp.zeros((columns + extra, 2 * columns), F32)
-    for z in range(depth):
-        loads[2 * z].wait()
-        wide[0:columns, 0:height, :] = basis_in[z].astype(F32)
-        loads[2 * z + 1].wait()
-        wide[columns:2 * columns, 0:height, :] = image_in[z].astype(F32)
+    pitch = height + PITCH_EXTRA
+
+    def gram_layer(z, gram):
+        for which, (source, target) in enumerate(((basis_ref, basis_in), (image_ref, image_in))):
+            pltpu.make_async_copy(
+                source.at[:, z], target.at[z], in_sems.at[2 * z + which]).wait()
+            for c in range(columns):
+                wide[pl.ds((which * columns + c) * pitch, height), :] = target[z, c].astype(F32)
         for g in range(groups):
             turned_rows = []
             for y in range(g * GROUP, (g + 1) * GROUP):
-                both = flat[pl.ds(y, 2 * columns, stride=PITCH), :].astype(BF16)
+                both = wide[pl.ds(y, 2 * columns, stride=pitch), :].astype(BF16)
                 rows_of_basis[z, y] = both[0:columns + extra]
                 turned_rows.append(both)
             stacked = jnp.concatenate(turned_rows, axis=1)
             gram = gram + dot_nt(stacked[low:], stacked)
+        return gram
+
+    gram = lax.fori_loop(
+        0, depth, gram_layer, jnp.zeros((columns + extra, 2 * columns), F32))
 
     source_row = lax.broadcasted_iota(jnp.int32, (2 * columns, LANES), 0)
     lane = lax.broadcasted_iota(jnp.int32, (2 * columns, LANES), 1)
-    wanted = jnp.where(
-        lane < columns, lane + columns, jnp.broadcast_to(picked_ref[...], (2 * columns, LANES)))
-    select = jnp.where(source_row == wanted, 1.0, 0.0).astype(BF16)
+    column = lax.broadcasted_iota(jnp.int32, (2 * columns, count), 0)
+    chosen_one = jnp.where(column == picked_ref[...], 1.0, 0.0).astype(BF16)
+    place = lax.broadcasted_iota(jnp.int32, (count, LANES), 1) - columns
+    place = jnp.where(
+        place == lax.broadcasted_iota(jnp.int32, (count, LANES), 0), 1.0, 0.0).astype(BF16)
+    select = jnp.dot(chosen_one, place, preferred_element_type=F32)
+    select = jnp.where(
+        jnp.logical_and(lane < columns, source_row == lane + columns), 1.0, select).astype(BF16)
     high, rest = gram.astype(BF16), gram
     augmented = jnp.dot(high, select, preferred_element_type=F32)
     for _ in range(2):
@@ -337,11 +347,11 @@
     app_store.wait()
 
 
-def final_kernel(inverse_ref, rec_ref, app_ref, rec_out, app_out):
+def final_kernel(inverse_ref, rec_ref, app_ref, rec_out, app_out, rec_wide, app_wide):
     height, count, width = rec_ref.shape
     factors = inverse_ref[...][:, 0:3 * count].astype(BF16)
-    for source, target in ((rec_ref, rec_out), (app_ref, app_out)):
-        flat = target.reshape(count * height, width)
+    pitch = height + PITCH_EXTRA
+    for source, target, wide in ((rec_ref, rec_out, rec_wide), (app_ref, app_out, app_wide)):
         for g in range(height // GROUP):
             values = jnp.concatenate(
                 [source[y] for y in range(g * GROUP, (g + 1) * GROUP)], axis=1)
@@ -349,8 +359,10 @@
             result = jnp.dot(
                 factors, jnp.concatenate([high, rest, high], axis=0), preferred_element_type=F32)
             for i in range(GROUP):
-                flat[pl.ds(g * GROUP + i, count, stride=height), :] = (
+                wide[pl.ds(g * GROUP + i, count, stride=pitch), :] = (
                     result[:, i * width:(i + 1) * width])
+        for k in range(count):
+            target[k] = wide[pl.ds(k * pitch, height), :]
 
 
 def local(slabs, pencils, basis, image, material, picked):
@@ -359,8 +371,6 @@
     extra = 16 - columns % 16 if columns % 16 else 0
     padded = columns + extra
     cells = depth * height * width * slabs * pencils
-    lanes = jnp.pad(
-        picked[None, :], ((0, 0), (columns, LANES - columns - count)), constant_values=-1)
 
     def sum_scratch(rows):
         return [
@@ -385,7 +395,7 @@
         scratch_shapes=[
             pltpu.VMEM((depth, columns, height, width), BF16),
             pltpu.VMEM((depth, columns, height, width), BF16),
-            pltpu.VMEM((2 * columns, PITCH, width), F32),
+            pltpu.VMEM((2 * columns * (height + PITCH_EXTRA), width), F32),
             pltpu.VMEM((depth, height, padded, width), BF16),
             pltpu.VMEM((count, padded), BF16),
             pltpu.VMEM((depth + 2, height + 2, count, width), F32),
@@ -408,7 +418,7 @@
         compiler_params=pltpu.CompilerParams(
             collective_id=0, has_side_effects=True, vmem_limit_bytes=56 * 1024 * 1024),
         name="recycle_update",
-    )(basis, image, material, lanes)
+    )(basis, image, material, picked[None, :])
     whole = pl.BlockSpec((None, height, count, width), lambda z: (z, 0, 0, 0))
     placed = pl.BlockSpec((count, None, height, width), lambda z: (0, z, 0, 0))
     out = jax.ShapeDtypeStruct((count, depth, height, width), F32)
@@ -418,7 +428,8 @@
         out_shape=(out, out),
         in_specs=[pl.BlockSpec((count, LANES), lambda z: (0, 0)), whole, whole],
         out_specs=(placed, placed),
-        compiler_params=pltpu.CompilerParams(vmem_limit_bytes=32 * 1024 * 1024),
+        scratch_shapes=[pltpu.VMEM((count * (height + PITCH_EXTRA), width), F32)] * 2,
+        compiler_params=pltpu.CompilerParams(vmem_limit_bytes=60 * 1024 * 1024),
         name="times_inverse",
     )(inverse, rec, app)
 

time: 69.5 us -> 64 us (0.921)
  local copies, waits for them, and re-layouts: 6.32 us -> 0 us
  Pallas kernels: 62.2 us -> 63 us
    unnamed x6 -> x0, local copies, waits for them, and re-layouts: 5.09 us -> none
    pallas_call x1, Pallas kernels: 8.01 us -> 10.2 us  [local(): pl.pallas_call(final_kernel, grid=(depth,), out_shape=(out, out), in_spec...]
    pallas_call x1, Pallas kernels: 54.2 us -> 52.8 us  [local(): pl.pallas_call(functools.partial(main_kernel, slabs, pencils, count, cell...]
    pad x1 -> x0, local copies, waits for them, and re-layouts: 1.24 us -> none  [local(): jnp.pad(picked[None, :], ((0, 0), (columns, LANES - columns - count)), co...]
where the time goes in v1:
time: 64 us; the launch traced here: 63.7 us
  Pallas kernels  63 us (98%)
  between operations  0.64 us (1%)
    pallas_call x1, Pallas kernels, local(): pl.pallas_call(functools.partial(main_kernel, slabs, pencils, count, cell...  52.8 us
    pallas_call x1, Pallas kernels, local(): pl.pallas_call(final_kernel, grid=(depth,), out_shape=(out, out), in_spec...  10.2 us

profile of v1, /device:TPU:0, one launch (start us, length us, event | category | flops | bytes accessed | tf_op | source)
XLA Modules:
  0.0 63.7 jit_solution(1954676531183704704)
XLA Ops:
  0.6 52.8 %recycle_update.1 = (f32[8,32,32,128]{3,2,1,0:T(8,128)}, f32[8,32,32,128]{3,2,1,0:T(8,128)}, f32[32,128]{1,0:T(8,128)}) custom-call(bf16[88,8,32,128]{3,2,1,0:T(8,128)(2,1)} %basis_ref.1, bf16[88,8,32,128]{3,2,1,0:T(8,128)(2,1)} %image_ref.1, s32[8,32,128]{2,1,0:T(8,128)} %material_ref.1, s32[1,32]{1,0:T(1,128)} %bitcast.1), custom_call_target="tpu_custom_call" | custom-call | tf_op jit(solution)/shard_map/recycle_update/pallas_call | solution.py:390
  53.4 10.2 %times_inverse.1 = (f32[32,8,32,128]{3,2,1,0:T(8,128)}, f32[32,8,32,128]{3,2,1,0:T(8,128)}) custom-call(f32[32,128]{1,0:T(8,128)} %get-tuple-element.5.inverse_ref, f32[8,32,32,128]{3,2,1,0:T(8,128)} %get-tuple-element.6.rec_ref, f32[8,32,32,128]{3,2,1,0:T(8,128)} %get-tuple-element.7.app_ref), custom_call_target="tpu_custom_call" | custom-call | tf_op jit(solution)/shard_map/times_inverse/pallas_call | solution.py:425

commit v2 on v1

--- a/solution.py
+++ b/solution.py
@@ -24,6 +24,13 @@
     return high, (value - high.astype(F32)).astype(BF16)
 
 
+def reciprocal(value):
+    guess = pl.reciprocal(value, approx=True)
+    for _ in range(2):
+        guess = guess + guess * (1.0 - value * guess)
+    return guess
+
+
 def splat(tile, column):
     return jnp.broadcast_to(tile[:, column:column + 1], tile.shape)
 
@@ -51,7 +58,7 @@
     for step in range(unknowns // 4):
         block, first, columns, rows, pivots = pivot_block(tiles, step)
         for j in range(4):
-            scale = 1.0 / pivots[j][j]
+            scale = reciprocal(pivots[j][j])
             rows[j] = rows[j] * scale
             for c in range(j + 1, 4):
                 pivots[j][c] = pivots[j][c] * scale
@@ -77,7 +84,7 @@
         block, first, columns, rows, pivots = pivot_block(tiles, step)
         done = []
         for j in range(4):
-            scale = 1.0 / pivots[j][j]
+            scale = reciprocal(pivots[j][j])
             done.append(rows[j] * lax.rsqrt(pivots[j][j]))
             rows[j] = rows[j] * scale
             for c in range(j + 1, 4):
@@ -157,13 +164,33 @@
         copy.wait_send()
 
 
+def gather_sum(value, slots, send, recv, axis, count):
+    me = lax.axis_index(axis)
+    place = {"slab": lax.axis_index("slab"), "pencil": lax.axis_index("pencil")}
+    slots[me] = value
+    copies = []
+    for d in range(1, count):
+        copies.append(pltpu.make_async_remote_copy(
+            src_ref=slots.at[me], dst_ref=slots.at[me],
+            send_sem=send.at[d - 1], recv_sem=recv.at[d - 1],
+            device_id={**place, axis: lax.rem(me + d, count)}, device_id_type=MESH))
+    for copy in copies:
+        copy.start()
+    for copy in copies:
+        copy.wait_recv()
+    total = slots[0]
+    for s in range(1, count):
+        total = total + slots[s]
+    return total, copies
+
+
 def main_kernel(
     slabs, pencils, count, cells,
     basis_ref, image_ref, material_ref, picked_ref,
     rec_out, app_out, inverse_out,
-    basis_in, image_in, wide, rows_of_basis, weights, rec, app, factor,
+    basis_in, image_in, wide, rows_of_basis, weights, rec, rec_halves, app_halves, factor,
     z_send, z_halo, y_send, y_halo,
-    part1, slots1, gathered1, total1, part2, slots2, gathered2, total2, turned,
+    part1, slots1, gathered1, total1, slots2, gathered2, turned,
     in_sems, out_sems, halo_send, halo_recv, *sum_sems,
 ):
     columns, depth, height, width = basis_in.shape[1], *basis_in.shape[:1], *basis_in.shape[2:]
@@ -281,9 +308,6 @@
     pl.when(sends[2])(y_copies[0].start)
     y_send[1] = rec[1:depth + 1, 1].astype(BF16)
     pl.when(sends[3])(y_copies[1].start)
-    rec_store = pltpu.make_async_copy(
-        rec.at[pl.ds(1, depth), pl.ds(1, height)], rec_out, out_sems.at[0])
-    rec_store.start()
 
     lanes = lax.broadcasted_iota(jnp.int32, (count, width), 1)
 
@@ -297,12 +321,18 @@
                 beside = beside + jnp.where(
                     lanes == width - 1, 0.0, pltpu.roll(center, width - 1, 1))
                 value = factor[z, y:y + 1, :] * center - beside
-                app[z, y] = value
                 values.append(value)
             high, rest = split(jnp.concatenate(values, axis=1))
             both = jnp.concatenate([high, rest], axis=0)
+            for i in range(GROUP):
+                app_halves[z, g * GROUP + i] = both[:, i * width:(i + 1) * width]
             normal = normal + dot_nt(both, both)
         return normal
+
+    def halve_layer(z):
+        for y in range(height):
+            high, rest = split(rec[z + 1, y + 1])
+            rec_halves[z, y] = jnp.concatenate([high, rest], axis=0)
 
     for side, (take, send) in enumerate(zip(takes[2:], sends[2:])):
         pl.when(take)(y_copies[side].wait_recv)
@@ -313,6 +343,9 @@
 
         rec[1:depth + 1, 0 if side == 0 else height + 1] = y_halo[side].astype(F32)
     normal = lax.fori_loop(1, depth - 1, applied_layer, jnp.zeros((2 * count, 2 * count), F32))
+    pl.loop(0, depth)(halve_layer)
+    rec_store = pltpu.make_async_copy(rec_halves, rec_out, out_sems.at[0])
+    rec_store.start()
     for side, take in enumerate(takes[:2]):
         pl.when(take)(z_copies[side].wait_recv)
 
@@ -322,18 +355,28 @@
 
         rec[0 if side == 0 else depth + 1, 1:height + 1] = z_halo[side].astype(F32)
         normal = applied_layer(0 if side == 0 else depth - 1, normal)
-    app_store = pltpu.make_async_copy(app, app_out, out_sems.at[1])
+    app_store = pltpu.make_async_copy(app_halves, app_out, out_sems.at[1])
     app_store.start()
 
     turned[0:2 * count, 0:2 * count] = normal
     halves = turned[0:count, :] + turned[count:2 * count, :]
-    part2[...] = halves + pltpu.roll(halves, LANES - count, 1)
-    all_sum(part2, slots2, gathered2, total2, sum_sems[6:12], slabs, pencils)
+    halves = halves + pltpu.roll(halves, LANES - count, 1)
+    lane = lax.broadcasted_iota(jnp.int32, (8, LANES), 1)
+    packed = halves[0:8]
+    for t in range(1, count // 8):
+        packed = jnp.where(
+            lane < t * count, packed, pltpu.roll(halves[8 * t:8 * (t + 1)], t * count, 1))
+    packed, pencil_copies = gather_sum(
+        packed, slots2, sum_sems[6], sum_sems[7], "pencil", pencils)
+    packed, slab_copies = gather_sum(
+        packed, gathered2, sum_sems[8], sum_sems[9], "slab", slabs)
+    total2 = jnp.concatenate(
+        [packed] + [pltpu.roll(packed, LANES - t * count, 1) for t in range(1, count // 8)], axis=0)
 
     row = lax.broadcasted_iota(jnp.int32, (count, LANES), 0)
     lane = lax.broadcasted_iota(jnp.int32, (count, LANES), 1)
     matrix = jnp.where(
-        lane < count, total2[...] * (1.0 / cells), jnp.where(lane == row + count, 1.0, 0.0))
+        lane < count, total2 * (1.0 / cells), jnp.where(lane == row + count, 1.0, 0.0))
     tiles = eliminate([matrix[8 * t:8 * (t + 1), :] for t in range(count // 8)], count)
     inverse = pltpu.roll(jnp.concatenate(tiles, axis=0), LANES - count, 1)
     inverse = jnp.where(lane <= row, inverse, 0.0)
@@ -341,28 +384,28 @@
     rest = (inverse - high).astype(BF16).astype(F32)
     inverse_out[...] = high + pltpu.roll(high, count, 1) + pltpu.roll(rest, 2 * count, 1)
 
+    for copy in pencil_copies + slab_copies:
+        copy.wait_send()
     for copy, send in zip(z_copies + y_copies, sends):
         pl.when(send)(copy.wait_send)
     rec_store.wait()
     app_store.wait()
 
 
-def final_kernel(inverse_ref, rec_ref, app_ref, rec_out, app_out, rec_wide, app_wide):
-    height, count, width = rec_ref.shape
+def final_kernel(inverse_ref, rec_ref, app_ref, rec_out, app_out):
+    height, count, width = rec_ref.shape[0], rec_ref.shape[1] // 2, rec_ref.shape[2]
     factors = inverse_ref[...][:, 0:3 * count].astype(BF16)
-    pitch = height + PITCH_EXTRA
-    for source, target, wide in ((rec_ref, rec_out, rec_wide), (app_ref, app_out, app_wide)):
+    for source, target in ((rec_ref, rec_out), (app_ref, app_out)):
+        flat = target.reshape(count * height, width)
         for g in range(height // GROUP):
             values = jnp.concatenate(
                 [source[y] for y in range(g * GROUP, (g + 1) * GROUP)], axis=1)
-            high, rest = split(values)
             result = jnp.dot(
-                factors, jnp.concatenate([high, rest, high], axis=0), preferred_element_type=F32)
+                factors, jnp.concatenate([values, values[0:count]], axis=0),
+                preferred_element_type=F32)
             for i in range(GROUP):
-                wide[pl.ds(g * GROUP + i, count, stride=pitch), :] = (
+                flat[pl.ds(g * GROUP + i, count, stride=height), :] = (
                     result[:, i * width:(i + 1) * width])
-        for k in range(count):
-            target[k] = wide[pl.ds(k * pitch, height), :]
 
 
 def local(slabs, pencils, basis, image, material, picked):
@@ -380,13 +423,12 @@
             pltpu.VMEM((rows, LANES), F32),
         ]
 
-    def sum_sems():
-        return [pltpu.SemaphoreType.DMA((n - 1,)) for n in (
-            pencils, pencils, slabs, slabs, pencils, pencils)]
+    def sum_sems(*counts):
+        return [pltpu.SemaphoreType.DMA((n - 1,)) for n in counts]
 
     in_vmem = pl.BlockSpec(memory_space=pltpu.VMEM)
     anywhere = pl.BlockSpec(memory_space=pl.ANY)
-    turned_shape = jax.ShapeDtypeStruct((depth, height, count, width), F32)
+    turned_shape = jax.ShapeDtypeStruct((depth, height, 2 * count, width), BF16)
     rec, app, inverse = pl.pallas_call(
         functools.partial(main_kernel, slabs, pencils, count, cells),
         out_shape=(turned_shape, turned_shape, jax.ShapeDtypeStruct((count, LANES), F32)),
@@ -399,27 +441,29 @@
             pltpu.VMEM((depth, height, padded, width), BF16),
             pltpu.VMEM((count, padded), BF16),
             pltpu.VMEM((depth + 2, height + 2, count, width), F32),
-            pltpu.VMEM((depth, height, count, width), F32),
+            pltpu.VMEM((depth, height, 2 * count, width), BF16),
+            pltpu.VMEM((depth, height, 2 * count, width), BF16),
             pltpu.VMEM((depth, height, width), F32),
             pltpu.VMEM((2, height, count, width), BF16),
             pltpu.VMEM((2, height, count, width), BF16),
             pltpu.VMEM((2, depth, count, width), BF16),
             pltpu.VMEM((2, depth, count, width), BF16),
             *sum_scratch(padded),
-            *sum_scratch(count),
+            pltpu.VMEM((pencils, 8, LANES), F32),
+            pltpu.VMEM((slabs, 8, LANES), F32),
             pltpu.VMEM((LANES, LANES), F32),
             pltpu.SemaphoreType.DMA((2 * depth,)),
             pltpu.SemaphoreType.DMA((2,)),
             pltpu.SemaphoreType.DMA((4,)),
             pltpu.SemaphoreType.DMA((4,)),
-            *sum_sems(),
-            *sum_sems(),
+            *sum_sems(pencils, pencils, slabs, slabs, pencils, pencils),
+            *sum_sems(pencils, pencils, slabs, slabs),
         ],
         compiler_params=pltpu.CompilerParams(
             collective_id=0, has_side_effects=True, vmem_limit_bytes=56 * 1024 * 1024),
         name="recycle_update",
     )(basis, image, material, picked[None, :])
-    whole = pl.BlockSpec((None, height, count, width), lambda z: (z, 0, 0, 0))
+    whole = pl.BlockSpec((None, height, 2 * count, width), lambda z: (z, 0, 0, 0))
     placed = pl.BlockSpec((count, None, height, width), lambda z: (0, z, 0, 0))
     out = jax.ShapeDtypeStruct((count, depth, height, width), F32)
     return pl.pallas_call(
@@ -428,7 +472,6 @@
         out_shape=(out, out),
         in_specs=[pl.BlockSpec((count, LANES), lambda z: (0, 0)), whole, whole],
         out_specs=(placed, placed),
-        scratch_shapes=[pltpu.VMEM((count * (height + PITCH_EXTRA), width), F32)] * 2,
         compiler_params=pltpu.CompilerParams(vmem_limit_bytes=60 * 1024 * 1024),
         name="times_inverse",
     )(inverse, rec, app)

time: 64 us -> 64.9 us (1.014)
  Pallas kernels: 63 us -> 63.9 us
    pallas_call x1, Pallas kernels: 10.2 us -> 11.3 us  [local(): pl.pallas_call(final_kernel, grid=(depth,), out_shape=(out, out), in_spec...]
where the time goes in v2:
time: 64.9 us; the launch traced here: 64.6 us
  Pallas kernels  63.9 us (98%)
    pallas_call x1, Pallas kernels, local(): pl.pallas_call(functools.partial(main_kernel, slabs, pencils, count, cell...  52.6 us
    pallas_call x1, Pallas kernels, local(): pl.pallas_call(final_kernel, grid=(depth,), out_shape=(out, out), in_spec...  11.3 us

profile of v2, /device:TPU:0, one launch (start us, length us, event | category | flops | bytes accessed | tf_op | source)
XLA Modules:
  0.0 64.6 jit_solution(10208074400219524194)
XLA Ops:
  0.6 52.6 %recycle_update.1 = (bf16[8,32,64,128]{3,2,1,0:T(8,128)(2,1)}, bf16[8,32,64,128]{3,2,1,0:T(8,128)(2,1)}, f32[32,128]{1,0:T(8,128)}) custom-call(bf16[88,8,32,128]{3,2,1,0:T(8,128)(2,1)} %basis_ref.1, bf16[88,8,32,128]{3,2,1,0:T(8,128)(2,1)} %image_ref.1, s32[8,32,128]{2,1,0:T(8,128)} %material_ref.1, s32[1,32]{1,0:T(1,128)} %bitcast.1), custom_call_target="tpu_custom_call" | custom-call | tf_op jit(solution)/shard_map/recycle_update/pallas_call | solution.py:432
  53.3 11.3 %times_inverse.1 = (f32[32,8,32,128]{3,2,1,0:T(8,128)}, f32[32,8,32,128]{3,2,1,0:T(8,128)}) custom-call(f32[32,128]{1,0:T(8,128)} %get-tuple-element.5.inverse_ref, bf16[8,32,64,128]{3,2,1,0:T(8,128)(2,1)} %get-tuple-element.6.rec_ref, bf16[8,32,64,128]{3,2,1,0:T(8,128)(2,1)} %get-tuple-element.7.app_ref), custom_call_target="tpu_custom_call" | custom-call | tf_op jit(solution)/shard_map/times_inverse/pallas_call | solution.py:469

commit v3 on v2

--- a/solution.py
+++ b/solution.py
@@ -184,26 +184,88 @@
     return total, copies
 
 
+def paired(factors):
+    none = jnp.zeros_like(factors)
+    return jnp.concatenate([
+        jnp.concatenate([factors, none], axis=1), jnp.concatenate([none, factors], axis=1)], axis=0)
+
+
+def pair_product(factors, rows, keep, width):
+    half = GROUP // 2
+    sides = [jnp.concatenate([rows(i) for i in range(s * half, (s + 1) * half)], axis=1)
+             for s in range(2)]
+    if keep:
+        sides = [jnp.concatenate([side, side[0:keep]], axis=0) for side in sides]
+    result = jnp.dot(factors, jnp.concatenate(sides, axis=0), preferred_element_type=F32)
+    count = result.shape[0] // 2
+    return [result[s * count:(s + 1) * count, i * width:(i + 1) * width]
+            for s in range(2) for i in range(half)]
+
+
+def gram_kernel(basis_ref, image_ref, picked_ref, rows_out, sums_out, wide, gram):
+    columns, height, width = basis_ref.shape
+    count = picked_ref.shape[1]
+    padded = rows_out.shape[1]
+    low = 2 * columns - padded
+    pitch = height + PITCH_EXTRA
+    z = pl.program_id(0)
+
+    @pl.when(z == 0)
+    def _():
+        gram[...] = jnp.zeros_like(gram)
+
+    for which, source in enumerate((basis_ref, image_ref)):
+        for c in range(columns):
+            wide[pl.ds((which * columns + c) * pitch, height), :] = source[c].astype(F32)
+    total = gram[...]
+    for g in range(height // GROUP):
+        turned_rows = []
+        for y in range(g * GROUP, (g + 1) * GROUP):
+            both = wide[pl.ds(y, 2 * columns, stride=pitch), :].astype(BF16)
+            rows_out[y] = both[0:padded]
+            turned_rows.append(both)
+        stacked = jnp.concatenate(turned_rows, axis=1)
+        total = total + dot_nt(stacked[low:], stacked)
+    gram[...] = total
+
+    @pl.when(z == pl.num_programs(0) - 1)
+    def _():
+        source_row = lax.broadcasted_iota(jnp.int32, (2 * columns, LANES), 0)
+        lane = lax.broadcasted_iota(jnp.int32, (2 * columns, LANES), 1)
+        column = lax.broadcasted_iota(jnp.int32, (2 * columns, count), 0)
+        chosen_one = jnp.where(column == picked_ref[...], 1.0, 0.0).astype(BF16)
+        place = lax.broadcasted_iota(jnp.int32, (count, LANES), 1) - columns
+        place = jnp.where(
+            place == lax.broadcasted_iota(jnp.int32, (count, LANES), 0), 1.0, 0.0).astype(BF16)
+        select = jnp.dot(chosen_one, place, preferred_element_type=F32)
+        select = jnp.where(
+            jnp.logical_and(lane < columns, source_row == lane + columns), 1.0, select)
+        select = select.astype(BF16)
+        high, rest = total.astype(BF16), total
+        augmented = jnp.dot(high, select, preferred_element_type=F32)
+        for _ in range(2):
+            rest = rest - high.astype(F32)
+            high = rest.astype(BF16)
+            augmented = augmented + jnp.dot(high, select, preferred_element_type=F32)
+        sums_out[...] = augmented
+
+
 def main_kernel(
-    slabs, pencils, count, cells,
-    basis_ref, image_ref, material_ref, picked_ref,
+    slabs, pencils, count, cells, columns,
+    rows_ref, part1, material_ref,
     rec_out, app_out, inverse_out,
-    basis_in, image_in, wide, rows_of_basis, weights, rec, rec_halves, app_halves, factor,
+    rows_of_basis, weights, rec, rec_halves, app_halves, factor,
     z_send, z_halo, y_send, y_halo,
-    part1, slots1, gathered1, total1, slots2, gathered2, turned,
-    in_sems, out_sems, halo_send, halo_recv, *sum_sems,
+    slots1, gathered1, total1, slots2, gathered2, turned,
+    in_sem, out_sems, halo_send, halo_recv, *sum_sems,
 ):
-    columns, depth, height, width = basis_in.shape[1], *basis_in.shape[:1], *basis_in.shape[2:]
+    depth, height, padded, width = rows_of_basis.shape
+    extra = padded - columns
     groups = height // GROUP
     slab, pencil = lax.axis_index("slab"), lax.axis_index("pencil")
 
-    loads = []
-    for z in range(depth):
-        for which, (source, target) in enumerate(((basis_ref, basis_in), (image_ref, image_in))):
-            loads.append(pltpu.make_async_copy(
-                source.at[:, z], target.at[z], in_sems.at[2 * z + which]))
-    for load in loads:
-        load.start()
+    load = pltpu.make_async_copy(rows_ref, rows_of_basis, in_sem)
+    load.start()
 
     barrier = pltpu.get_barrier_semaphore()
     for d in range(1, pencils):
@@ -220,46 +282,6 @@
         material == 0, 0.3,
         jnp.where(material == 1, 0.9, jnp.where(material == 2, 1.6, 2.5))).astype(F32)
 
-    extra = 16 - columns % 16 if columns % 16 else 0
-    low = columns - extra
-    pitch = height + PITCH_EXTRA
-
-    def gram_layer(z, gram):
-        for which, (source, target) in enumerate(((basis_ref, basis_in), (image_ref, image_in))):
-            pltpu.make_async_copy(
-                source.at[:, z], target.at[z], in_sems.at[2 * z + which]).wait()
-            for c in range(columns):
-                wide[pl.ds((which * columns + c) * pitch, height), :] = target[z, c].astype(F32)
-        for g in range(groups):
-            turned_rows = []
-            for y in range(g * GROUP, (g + 1) * GROUP):
-                both = wide[pl.ds(y, 2 * columns, stride=pitch), :].astype(BF16)
-                rows_of_basis[z, y] = both[0:columns + extra]
-                turned_rows.append(both)
-            stacked = jnp.concatenate(turned_rows, axis=1)
-            gram = gram + dot_nt(stacked[low:], stacked)
-        return gram
-
-    gram = lax.fori_loop(
-        0, depth, gram_layer, jnp.zeros((columns + extra, 2 * columns), F32))
-
-    source_row = lax.broadcasted_iota(jnp.int32, (2 * columns, LANES), 0)
-    lane = lax.broadcasted_iota(jnp.int32, (2 * columns, LANES), 1)
-    column = lax.broadcasted_iota(jnp.int32, (2 * columns, count), 0)
-    chosen_one = jnp.where(column == picked_ref[...], 1.0, 0.0).astype(BF16)
-    place = lax.broadcasted_iota(jnp.int32, (count, LANES), 1) - columns
-    place = jnp.where(
-        place == lax.broadcasted_iota(jnp.int32, (count, LANES), 0), 1.0, 0.0).astype(BF16)
-    select = jnp.dot(chosen_one, place, preferred_element_type=F32)
-    select = jnp.where(
-        jnp.logical_and(lane < columns, source_row == lane + columns), 1.0, select).astype(BF16)
-    high, rest = gram.astype(BF16), gram
-    augmented = jnp.dot(high, select, preferred_element_type=F32)
-    for _ in range(2):
-        rest = rest - high.astype(F32)
-        high = rest.astype(BF16)
-        augmented = augmented + jnp.dot(high, select, preferred_element_type=F32)
-    part1[...] = augmented
 
     pl.semaphore_wait(barrier, slabs + pencils - 2)
     all_sum(part1, slots1, gathered1, total1, sum_sems[0:6], slabs, pencils)
@@ -269,15 +291,15 @@
     turned[...] = jnp.zeros_like(turned)
     for t, tile in enumerate(tiles):
         turned[8 * t:8 * (t + 1), :] = tile
-    weights[...] = turned[...].T[columns:columns + count, 0:columns + extra].astype(BF16)
+    weights[...] = paired(turned[...].T[columns:columns + count, 0:padded]).astype(BF16)
+    load.wait()
 
     def recycle_layer(z):
         for g in range(groups):
-            cells_in = jnp.concatenate(
-                [rows_of_basis[z, y] for y in range(g * GROUP, (g + 1) * GROUP)], axis=1)
-            result = jnp.dot(weights[...], cells_in, preferred_element_type=F32)
+            results = pair_product(
+                weights[...], lambda i: rows_of_basis[z, g * GROUP + i], 0, width)
             for i in range(GROUP):
-                rec[z + 1, 1 + g * GROUP + i] = result[:, i * width:(i + 1) * width]
+                rec[z + 1, 1 + g * GROUP + i] = results[i]
 
     def z_copy(side, peer):
         return pltpu.make_async_remote_copy(
@@ -392,20 +414,17 @@
     app_store.wait()
 
 
-def final_kernel(inverse_ref, rec_ref, app_ref, rec_out, app_out):
+def final_kernel(inverse_ref, rec_ref, app_ref, rec_out, app_out, rec_wide, app_wide):
     height, count, width = rec_ref.shape[0], rec_ref.shape[1] // 2, rec_ref.shape[2]
-    factors = inverse_ref[...][:, 0:3 * count].astype(BF16)
-    for source, target in ((rec_ref, rec_out), (app_ref, app_out)):
-        flat = target.reshape(count * height, width)
+    factors = paired(inverse_ref[...][:, 0:3 * count]).astype(BF16)
+    pitch = height + PITCH_EXTRA
+    for source, target, wide in ((rec_ref, rec_out, rec_wide), (app_ref, app_out, app_wide)):
         for g in range(height // GROUP):
-            values = jnp.concatenate(
-                [source[y] for y in range(g * GROUP, (g + 1) * GROUP)], axis=1)
-            result = jnp.dot(
-                factors, jnp.concatenate([values, values[0:count]], axis=0),
-                preferred_element_type=F32)
+            results = pair_product(factors, lambda i: source[g * GROUP + i], count, width)
             for i in range(GROUP):
-                flat[pl.ds(g * GROUP + i, count, stride=height), :] = (
-                    result[:, i * width:(i + 1) * width])
+                wide[pl.ds(g * GROUP + i, count, stride=pitch), :] = results[i]
+        for k in range(count):
+            target[k] = wide[pl.ds(k * pitch, height), :]
 
 
 def local(slabs, pencils, basis, image, material, picked):
@@ -417,7 +436,6 @@
 
     def sum_scratch(rows):
         return [
-            pltpu.VMEM((rows, LANES), F32),
             pltpu.VMEM((pencils - 1, rows // pencils, LANES), F32),
             pltpu.VMEM((slabs, rows // pencils, LANES), F32),
             pltpu.VMEM((rows, LANES), F32),
@@ -429,17 +447,30 @@
     in_vmem = pl.BlockSpec(memory_space=pltpu.VMEM)
     anywhere = pl.BlockSpec(memory_space=pl.ANY)
     turned_shape = jax.ShapeDtypeStruct((depth, height, 2 * count, width), BF16)
+    column_block = pl.BlockSpec((columns, None, height, width), lambda z: (0, z, 0, 0))
+    rows, sums = pl.pallas_call(
+        gram_kernel,
+        grid=(depth,),
+        out_shape=(jax.ShapeDtypeStruct((depth, height, padded, width), BF16),
+                   jax.ShapeDtypeStruct((padded, LANES), F32)),
+        in_specs=[column_block, column_block, pl.BlockSpec((1, count), lambda z: (0, 0))],
+        out_specs=(pl.BlockSpec((None, height, padded, width), lambda z: (z, 0, 0, 0)),
+                   pl.BlockSpec((padded, LANES), lambda z: (0, 0))),
+        scratch_shapes=[
+            pltpu.VMEM((2 * columns * (height + PITCH_EXTRA), width), F32),
+            pltpu.VMEM((padded, 2 * columns), F32),
+        ],
+        compiler_params=pltpu.CompilerParams(vmem_limit_bytes=60 * 1024 * 1024),
+        name="gram_matrices",
+    )(basis, image, picked[None, :])
     rec, app, inverse = pl.pallas_call(
-        functools.partial(main_kernel, slabs, pencils, count, cells),
+        functools.partial(main_kernel, slabs, pencils, count, cells, columns),
         out_shape=(turned_shape, turned_shape, jax.ShapeDtypeStruct((count, LANES), F32)),
-        in_specs=[anywhere, anywhere, in_vmem, in_vmem],
+        in_specs=[anywhere, in_vmem, in_vmem],
         out_specs=(anywhere, anywhere, in_vmem),
         scratch_shapes=[
-            pltpu.VMEM((depth, columns, height, width), BF16),
-            pltpu.VMEM((depth, columns, height, width), BF16),
-            pltpu.VMEM((2 * columns * (height + PITCH_EXTRA), width), F32),
             pltpu.VMEM((depth, height, padded, width), BF16),
-            pltpu.VMEM((count, padded), BF16),
+            pltpu.VMEM((2 * count, 2 * padded), BF16),
             pltpu.VMEM((depth + 2, height + 2, count, width), F32),
             pltpu.VMEM((depth, height, 2 * count, width), BF16),
             pltpu.VMEM((depth, height, 2 * count, width), BF16),
@@ -452,7 +483,7 @@
             pltpu.VMEM((pencils, 8, LANES), F32),
             pltpu.VMEM((slabs, 8, LANES), F32),
             pltpu.VMEM((LANES, LANES), F32),
-            pltpu.SemaphoreType.DMA((2 * depth,)),
+            pltpu.SemaphoreType.DMA(()),
             pltpu.SemaphoreType.DMA((2,)),
             pltpu.SemaphoreType.DMA((4,)),
             pltpu.SemaphoreType.DMA((4,)),
@@ -460,9 +491,9 @@
             *sum_sems(pencils, pencils, slabs, slabs),
         ],
         compiler_params=pltpu.CompilerParams(
-            collective_id=0, has_side_effects=True, vmem_limit_bytes=56 * 1024 * 1024),
+            collective_id=0, has_side_effects=True, vmem_limit_bytes=60 * 1024 * 1024),
         name="recycle_update",
-    )(basis, image, material, picked[None, :])
+    )(rows, sums, material)
     whole = pl.BlockSpec((None, height, 2 * count, width), lambda z: (z, 0, 0, 0))
     placed = pl.BlockSpec((count, None, height, width), lambda z: (0, z, 0, 0))
     out = jax.ShapeDtypeStruct((count, depth, height, width), F32)
@@ -472,6 +503,7 @@
         out_shape=(out, out),
         in_specs=[pl.BlockSpec((count, LANES), lambda z: (0, 0)), whole, whole],
         out_specs=(placed, placed),
+        scratch_shapes=[pltpu.VMEM((count * (height + PITCH_EXTRA), width), F32)] * 2,
         compiler_params=pltpu.CompilerParams(vmem_limit_bytes=60 * 1024 * 1024),
         name="times_inverse",
     )(inverse, rec, app)

time: 64.9 us -> 70 us (1.079)
  Pallas kernels: 63.9 us -> 68.9 us
    pallas_call x0 -> x1, Pallas kernels: none -> 12.1 us  [local(): pl.pallas_call(gram_kernel, grid=(depth,), out_shape=(jax.ShapeDtypeStruc...]
    pallas_call x1, Pallas kernels: 52.6 us -> 46.2 us  [local(): pl.pallas_call(functools.partial(main_kernel, slabs, pencils, count, cell...]
    pallas_call x1, Pallas kernels: 11.3 us -> 10.6 us  [local(): pl.pallas_call(final_kernel, grid=(depth,), out_shape=(out, out), in_spec...]
where the time goes in v3:
time: 70 us; the launch traced here: 69.5 us
  Pallas kernels  68.9 us (98%)
    pallas_call x1, Pallas kernels, local(): pl.pallas_call(functools.partial(main_kernel, slabs, pencils, count, cell...  46.2 us
    pallas_call x1, Pallas kernels, local(): pl.pallas_call(gram_kernel, grid=(depth,), out_shape=(jax.ShapeDtypeStruc...  12.1 us
    pallas_call x1, Pallas kernels, local(): pl.pallas_call(final_kernel, grid=(depth,), out_shape=(out, out), in_spec...  10.6 us

profile of v3, /device:TPU:0, one launch (start us, length us, event | category | flops | bytes accessed | tf_op | source)
XLA Modules:
  0.0 69.5 jit_solution(11162894965411563327)
XLA Ops:
  0.6 12.1 %gram_matrices.1 = (bf16[8,32,96,128]{3,2,1,0:T(8,128)(2,1)}, f32[96,128]{1,0:T(8,128)}) custom-call(bf16[88,8,32,128]{3,2,1,0:T(8,128)(2,1)} %basis_ref.1, bf16[88,8,32,128]{3,2,1,0:T(8,128)(2,1)} %image_ref.1, s32[1,32]{1,0:T(1,128)} %bitcast.1), custom_call_target="tpu_custom_call" | custom-call | tf_op jit(solution)/shard_map/gram_matrices/pallas_call | solution.py:451
  12.7 46.2 %recycle_update.1 = (bf16[8,32,64,128]{3,2,1,0:T(8,128)(2,1)}, bf16[8,32,64,128]{3,2,1,0:T(8,128)(2,1)}, f32[32,128]{1,0:T(8,128)}) custom-call(bf16[8,32,96,128]{3,2,1,0:T(8,128)(2,1)} %get-tuple-element.7.rows_ref, f32[96,128]{1,0:T(8,128)} %get-tuple-element.8.part1, s32[8,32,128]{2,1,0:T(8,128)} %material_ref.1), custom_call_target="tpu_custom_call" | custom-call | tf_op jit(solution)/shard_map/recycle_update/pallas_call | solution.py:466
  58.9 10.6 %times_inverse.1 = (f32[32,8,32,128]{3,2,1,0:T(8,128)}, f32[32,8,32,128]{3,2,1,0:T(8,128)}) custom-call(f32[32,128]{1,0:T(8,128)} %get-tuple-element.9.inverse_ref, bf16[8,32,64,128]{3,2,1,0:T(8,128)(2,1)} %get-tuple-element.10.rec_ref, bf16[8,32,64,128]{3,2,1,0:T(8,128)(2,1)} %get-tuple-element.11.app_ref), custom_call_target="tpu_custom_call" | custom-call | tf_op jit(solution)/shard_map/times_inverse/pallas_call | solution.py:500

commit v4 on v2

--- a/solution.py
+++ b/solution.py
@@ -184,6 +184,24 @@
     return total, copies
 
 
+def paired(factors):
+    none = jnp.zeros_like(factors)
+    return jnp.concatenate([
+        jnp.concatenate([factors, none], axis=1), jnp.concatenate([none, factors], axis=1)], axis=0)
+
+
+def pair_product(factors, rows, keep, width):
+    half = GROUP // 2
+    sides = [jnp.concatenate([rows(i) for i in range(s * half, (s + 1) * half)], axis=1)
+             for s in range(2)]
+    if keep:
+        sides = [jnp.concatenate([side, side[0:keep]], axis=0) for side in sides]
+    result = jnp.dot(factors, jnp.concatenate(sides, axis=0), preferred_element_type=F32)
+    count = result.shape[0] // 2
+    return [result[s * count:(s + 1) * count, i * width:(i + 1) * width]
+            for s in range(2) for i in range(half)]
+
+
 def main_kernel(
     slabs, pencils, count, cells,
     basis_ref, image_ref, material_ref, picked_ref,
@@ -269,15 +287,15 @@
     turned[...] = jnp.zeros_like(turned)
     for t, tile in enumerate(tiles):
         turned[8 * t:8 * (t + 1), :] = tile
-    weights[...] = turned[...].T[columns:columns + count, 0:columns + extra].astype(BF16)
+    weights[...] = paired(
+        turned[...].T[columns:columns + count, 0:columns + extra]).astype(BF16)
 
     def recycle_layer(z):
         for g in range(groups):
-            cells_in = jnp.concatenate(
-                [rows_of_basis[z, y] for y in range(g * GROUP, (g + 1) * GROUP)], axis=1)
-            result = jnp.dot(weights[...], cells_in, preferred_element_type=F32)
+            results = pair_product(
+                weights[...], lambda i: rows_of_basis[z, g * GROUP + i], 0, width)
             for i in range(GROUP):
-                rec[z + 1, 1 + g * GROUP + i] = result[:, i * width:(i + 1) * width]
+                rec[z + 1, 1 + g * GROUP + i] = results[i]
 
     def z_copy(side, peer):
         return pltpu.make_async_remote_copy(
@@ -297,6 +315,12 @@
     sends = (slab < slabs - 1, slab > 0, pencil < pencils - 1, pencil > 0)
     takes = (slab > 0, slab < slabs - 1, pencil > 0, pencil < pencils - 1)
 
+    for side, y in enumerate((height - 1, 0)):
+        for first in range(0, depth, GROUP):
+            edge = pair_product(weights[...], lambda i: rows_of_basis[first + i, y], 0, width)
+            for i in range(GROUP):
+                y_send[side, first + i] = edge[i].astype(BF16)
+        pl.when(sends[2 + side])(y_copies[side].start)
     recycle_layer(depth - 1)
     z_send[0] = rec[depth, 1:height + 1].astype(BF16)
     pl.when(sends[0])(z_copies[0].start)
@@ -304,10 +328,6 @@
     z_send[1] = rec[1, 1:height + 1].astype(BF16)
     pl.when(sends[1])(z_copies[1].start)
     pl.loop(1, depth - 1)(recycle_layer)
-    y_send[0] = rec[1:depth + 1, height].astype(BF16)
-    pl.when(sends[2])(y_copies[0].start)
-    y_send[1] = rec[1:depth + 1, 1].astype(BF16)
-    pl.when(sends[3])(y_copies[1].start)
 
     lanes = lax.broadcasted_iota(jnp.int32, (count, width), 1)
 
@@ -334,7 +354,10 @@
             high, rest = split(rec[z + 1, y + 1])
             rec_halves[z, y] = jnp.concatenate([high, rest], axis=0)
 
-    for side, (take, send) in enumerate(zip(takes[2:], sends[2:])):
+    pl.loop(0, depth)(halve_layer)
+    rec_store = pltpu.make_async_copy(rec_halves, rec_out, out_sems.at[0])
+    rec_store.start()
+    for side, take in enumerate(takes[2:]):
         pl.when(take)(y_copies[side].wait_recv)
 
         @pl.when(jnp.logical_not(take))
@@ -343,9 +366,6 @@
 
         rec[1:depth + 1, 0 if side == 0 else height + 1] = y_halo[side].astype(F32)
     normal = lax.fori_loop(1, depth - 1, applied_layer, jnp.zeros((2 * count, 2 * count), F32))
-    pl.loop(0, depth)(halve_layer)
-    rec_store = pltpu.make_async_copy(rec_halves, rec_out, out_sems.at[0])
-    rec_store.start()
     for side, take in enumerate(takes[:2]):
         pl.when(take)(z_copies[side].wait_recv)
 
@@ -392,20 +412,17 @@
     app_store.wait()
 
 
-def final_kernel(inverse_ref, rec_ref, app_ref, rec_out, app_out):
+def final_kernel(inverse_ref, rec_ref, app_ref, rec_out, app_out, rec_wide, app_wide):
     height, count, width = rec_ref.shape[0], rec_ref.shape[1] // 2, rec_ref.shape[2]
-    factors = inverse_ref[...][:, 0:3 * count].astype(BF16)
-    for source, target in ((rec_ref, rec_out), (app_ref, app_out)):
-        flat = target.reshape(count * height, width)
+    factors = paired(inverse_ref[...][:, 0:3 * count]).astype(BF16)
+    pitch = height + PITCH_EXTRA
+    for source, target, wide in ((rec_ref, rec_out, rec_wide), (app_ref, app_out, app_wide)):
         for g in range(height // GROUP):
-            values = jnp.concatenate(
-                [source[y] for y in range(g * GROUP, (g + 1) * GROUP)], axis=1)
-            result = jnp.dot(
-                factors, jnp.concatenate([values, values[0:count]], axis=0),
-                preferred_element_type=F32)
+            results = pair_product(factors, lambda i: source[g * GROUP + i], count, width)
             for i in range(GROUP):
-                flat[pl.ds(g * GROUP + i, count, stride=height), :] = (
-                    result[:, i * width:(i + 1) * width])
+                wide[pl.ds(g * GROUP + i, count, stride=pitch), :] = results[i]
+        for k in range(count):
+            target[k] = wide[pl.ds(k * pitch, height), :]
 
 
 def local(slabs, pencils, basis, image, material, picked):
@@ -439,7 +456,7 @@
             pltpu.VMEM((depth, columns, height, width), BF16),
             pltpu.VMEM((2 * columns * (height + PITCH_EXTRA), width), F32),
             pltpu.VMEM((depth, height, padded, width), BF16),
-            pltpu.VMEM((count, padded), BF16),
+            pltpu.VMEM((2 * count, 2 * padded), BF16),
             pltpu.VMEM((depth + 2, height + 2, count, width), F32),
             pltpu.VMEM((depth, height, 2 * count, width), BF16),
             pltpu.VMEM((depth, height, 2 * count, width), BF16),
@@ -472,6 +489,7 @@
         out_shape=(out, out),
         in_specs=[pl.BlockSpec((count, LANES), lambda z: (0, 0)), whole, whole],
         out_specs=(placed, placed),
+        scratch_shapes=[pltpu.VMEM((count * (height + PITCH_EXTRA), width), F32)] * 2,
         compiler_params=pltpu.CompilerParams(vmem_limit_bytes=60 * 1024 * 1024),
         name="times_inverse",
     )(inverse, rec, app)

time: 64.9 us -> 64.6 us (level)
    pallas_call x1, Pallas kernels: 11.3 us -> 10.6 us  [local(): pl.pallas_call(final_kernel, grid=(depth,), out_shape=(out, out), in_spec...]
where the time goes in v4:
time: 64.6 us; the launch traced here: 64.2 us
  Pallas kernels  63.6 us (98%)
    pallas_call x1, Pallas kernels, local(): pl.pallas_call(functools.partial(main_kernel, slabs, pencils, count, cell...  53 us
    pallas_call x1, Pallas kernels, local(): pl.pallas_call(final_kernel, grid=(depth,), out_shape=(out, out), in_spec...  10.6 us

profile of v4, /device:TPU:0, one launch (start us, length us, event | category | flops | bytes accessed | tf_op | source)
XLA Modules:
  0.0 64.2 jit_solution(17871949151692661957)
XLA Ops:
  0.6 53.0 %recycle_update.1 = (bf16[8,32,64,128]{3,2,1,0:T(8,128)(2,1)}, bf16[8,32,64,128]{3,2,1,0:T(8,128)(2,1)}, f32[32,128]{1,0:T(8,128)}) custom-call(bf16[88,8,32,128]{3,2,1,0:T(8,128)(2,1)} %basis_ref.1, bf16[88,8,32,128]{3,2,1,0:T(8,128)(2,1)} %image_ref.1, s32[8,32,128]{2,1,0:T(8,128)} %material_ref.1, s32[1,32]{1,0:T(1,128)} %bitcast.1), custom_call_target="tpu_custom_call" | custom-call | tf_op jit(solution)/shard_map/recycle_update/pallas_call | solution.py:449
  53.6 10.6 %times_inverse.1 = (f32[32,8,32,128]{3,2,1,0:T(8,128)}, f32[32,8,32,128]{3,2,1,0:T(8,128)}) custom-call(f32[32,128]{1,0:T(8,128)} %get-tuple-element.5.inverse_ref, bf16[8,32,64,128]{3,2,1,0:T(8,128)(2,1)} %get-tuple-element.6.rec_ref, bf16[8,32,64,128]{3,2,1,0:T(8,128)(2,1)} %get-tuple-element.7.app_ref), custom_call_target="tpu_custom_call" | custom-call | tf_op jit(solution)/shard_map/times_inverse/pallas_call | solution.py:486

commit v5 on v4

--- a/solution.py
+++ b/solution.py
@@ -13,6 +13,7 @@
 GROUP = 8
 PITCH_EXTRA = 1
 LANES = 128
+PIVOTS = 8
 
 
 def dot_nt(a, b):
@@ -39,75 +40,67 @@
     return jnp.broadcast_to(tile[index:index + 1, :], tile.shape)
 
 
-def merge_rows(tile, rows, first):
+def merge_rows(tile, rows):
     index = lax.broadcasted_iota(jnp.int32, tile.shape, 0)
     for offset, row in enumerate(rows):
-        tile = jnp.where(index == first + offset, row, tile)
+        tile = jnp.where(index == offset, row, tile)
     return tile
 
 
 def pivot_block(tiles, step):
-    block, first = step // 2, 4 * (step % 2)
-    columns = [[splat(tile, 4 * step + j) for j in range(4)] for tile in tiles]
-    rows = [row_of(tiles[block], first + i) for i in range(4)]
-    pivots = [[row_of(columns[block][j], first + i) for j in range(4)] for i in range(4)]
-    return block, first, columns, rows, pivots
+    columns = [[splat(tile, PIVOTS * step + j) for j in range(PIVOTS)] for tile in tiles]
+    rows = [row_of(tiles[step], i) for i in range(PIVOTS)]
+    pivots = [[row_of(columns[step][j], i) for j in range(PIVOTS)] for i in range(PIVOTS)]
+    return columns, rows, pivots
 
 
 def solve_spd(tiles, unknowns):
-    for step in range(unknowns // 4):
-        block, first, columns, rows, pivots = pivot_block(tiles, step)
-        for j in range(4):
+    for step in range(unknowns // PIVOTS):
+        columns, rows, pivots = pivot_block(tiles, step)
+        for j in range(PIVOTS):
             scale = reciprocal(pivots[j][j])
             rows[j] = rows[j] * scale
-            for c in range(j + 1, 4):
+            for c in range(j + 1, PIVOTS):
                 pivots[j][c] = pivots[j][c] * scale
-            for i in range(4):
+            for i in range(PIVOTS):
                 if i != j:
                     factor = pivots[i][j]
                     rows[i] = rows[i] - factor * rows[j]
-                    for c in range(j + 1, 4):
+                    for c in range(j + 1, PIVOTS):
                         pivots[i][c] = pivots[i][c] - factor * pivots[j][c]
         updated = []
         for t, tile in enumerate(tiles):
-            for j in range(4):
+            for j in range(PIVOTS):
                 tile = tile - columns[t][j] * rows[j]
-            if t == block:
-                tile = merge_rows(tile, rows, first)
-            updated.append(tile)
+            updated.append(merge_rows(tile, rows) if t == step else tile)
         tiles = updated
     return tiles
 
 
 def eliminate(tiles, unknowns):
-    for step in range(unknowns // 4):
-        block, first, columns, rows, pivots = pivot_block(tiles, step)
+    for step in range(unknowns // PIVOTS):
+        columns, rows, pivots = pivot_block(tiles, step)
         done = []
-        for j in range(4):
+        for j in range(PIVOTS):
             scale = reciprocal(pivots[j][j])
             done.append(rows[j] * lax.rsqrt(pivots[j][j]))
             rows[j] = rows[j] * scale
-            for c in range(j + 1, 4):
+            for c in range(j + 1, PIVOTS):
                 pivots[j][c] = pivots[j][c] * scale
-            for i in range(4):
+            for i in range(PIVOTS):
                 if i != j:
                     factor = pivots[i][j]
                     rows[i] = rows[i] - factor * rows[j]
-                    for c in range(j + 1, 4):
+                    for c in range(j + 1, PIVOTS):
                         pivots[i][c] = pivots[i][c] - factor * pivots[j][c]
-        index = lax.broadcasted_iota(jnp.int32, tiles[0].shape, 0)
         updated = []
         for t, tile in enumerate(tiles):
-            if t < block:
-                updated.append(tile)
-                continue
-            changed = tile
-            for j in range(4):
-                changed = changed - columns[t][j] * rows[j]
-            if t == block:
-                changed = jnp.where(index >= first + 4, changed, tile)
-                changed = merge_rows(changed, done, first)
-            updated.append(changed)
+            if t == step:
+                tile = merge_rows(tile, done)
+            elif t > step:
+                for j in range(PIVOTS):
+                    tile = tile - columns[t][j] * rows[j]
+            updated.append(tile)
         tiles = updated
     return tiles
 
@@ -412,17 +405,44 @@
     app_store.wait()
 
 
-def final_kernel(inverse_ref, rec_ref, app_ref, rec_out, app_out, rec_wide, app_wide):
-    height, count, width = rec_ref.shape[0], rec_ref.shape[1] // 2, rec_ref.shape[2]
+def final_kernel(
+    inverse_ref, rec_ref, app_ref, rec_out, app_out,
+    rec_in, app_in, rec_turned, app_turned, rec_wide, app_wide, in_sems, out_sems,
+):
+    depth, height, both, width = rec_in.shape
+    count = both // 2
+    pitch = height + PITCH_EXTRA
+    arrays = ((rec_ref, rec_in, rec_wide, rec_turned, rec_out),
+              (app_ref, app_in, app_wide, app_turned, app_out))
+
+    def load(z, which):
+        return pltpu.make_async_copy(
+            arrays[which][0].at[z], arrays[which][1].at[z], in_sems.at[2 * z + which])
+
+    def store(z, which):
+        return pltpu.make_async_copy(
+            arrays[which][3].at[z], arrays[which][4].at[:, z], out_sems.at[2 * z + which])
+
+    for z in range(depth):
+        for which in range(2):
+            load(z, which).start()
     factors = paired(inverse_ref[...][:, 0:3 * count]).astype(BF16)
-    pitch = height + PITCH_EXTRA
-    for source, target, wide in ((rec_ref, rec_out, rec_wide), (app_ref, app_out, app_wide)):
-        for g in range(height // GROUP):
-            results = pair_product(factors, lambda i: source[g * GROUP + i], count, width)
-            for i in range(GROUP):
-                wide[pl.ds(g * GROUP + i, count, stride=pitch), :] = results[i]
-        for k in range(count):
-            target[k] = wide[pl.ds(k * pitch, height), :]
+
+    @pl.loop(0, depth)
+    def _(z):
+        for which, (_, source, wide, turned, _) in enumerate(arrays):
+            load(z, which).wait()
+            for g in range(height // GROUP):
+                results = pair_product(factors, lambda i: source[z, g * GROUP + i], count, width)
+                for i in range(GROUP):
+                    wide[pl.ds(g * GROUP + i, count, stride=pitch), :] = results[i]
+            for k in range(count):
+                turned[z, k] = wide[pl.ds(k * pitch, height), :]
+            store(z, which).start()
+
+    for z in range(depth):
+        for which in range(2):
+            store(z, which).wait()
 
 
 def local(slabs, pencils, basis, image, material, picked):
@@ -480,16 +500,19 @@
             collective_id=0, has_side_effects=True, vmem_limit_bytes=56 * 1024 * 1024),
         name="recycle_update",
     )(basis, image, material, picked[None, :])
-    whole = pl.BlockSpec((None, height, 2 * count, width), lambda z: (z, 0, 0, 0))
-    placed = pl.BlockSpec((count, None, height, width), lambda z: (0, z, 0, 0))
     out = jax.ShapeDtypeStruct((count, depth, height, width), F32)
     return pl.pallas_call(
         final_kernel,
-        grid=(depth,),
         out_shape=(out, out),
-        in_specs=[pl.BlockSpec((count, LANES), lambda z: (0, 0)), whole, whole],
-        out_specs=(placed, placed),
-        scratch_shapes=[pltpu.VMEM((count * (height + PITCH_EXTRA), width), F32)] * 2,
+        in_specs=[in_vmem, anywhere, anywhere],
+        out_specs=(anywhere, anywhere),
+        scratch_shapes=[
+            *[pltpu.VMEM((depth, height, 2 * count, width), BF16)] * 2,
+            *[pltpu.VMEM((depth, count, height, width), F32)] * 2,
+            *[pltpu.VMEM((count * (height + PITCH_EXTRA), width), F32)] * 2,
+            pltpu.SemaphoreType.DMA((2 * depth,)),
+            pltpu.SemaphoreType.DMA((2 * depth,)),
+        ],
         compiler_params=pltpu.CompilerParams(vmem_limit_bytes=60 * 1024 * 1024),
         name="times_inverse",
     )(inverse, rec, app)

time: 64.6 us -> 59.9 us (0.927)
  Pallas kernels: 63.6 us -> 59 us
    pallas_call x1, Pallas kernels: 10.6 us -> 7.53 us  [local(): pl.pallas_call(final_kernel, out_shape=(out, out), in_specs=[in_vmem, any...]
    pallas_call x1, Pallas kernels: 53 us -> 51.5 us  [local(): pl.pallas_call(functools.partial(main_kernel, slabs, pencils, count, cell...]
where the time goes in v5:
time: 59.9 us; the launch traced here: 59.7 us
  Pallas kernels  59 us (98%)
  between operations  0.64 us (1%)
    pallas_call x1, Pallas kernels, local(): pl.pallas_call(functools.partial(main_kernel, slabs, pencils, count, cell...  51.5 us
    pallas_call x1, Pallas kernels, local(): pl.pallas_call(final_kernel, out_shape=(out, out), in_specs=[in_vmem, any...  7.53 us

profile of v5, /device:TPU:0, one launch (start us, length us, event | category | flops | bytes accessed | tf_op | source)
XLA Modules:
  0.0 59.7 jit_solution(1673971551724747301)
XLA Ops:
  0.6 51.5 %recycle_update.1 = (bf16[8,32,64,128]{3,2,1,0:T(8,128)(2,1)}, bf16[8,32,64,128]{3,2,1,0:T(8,128)(2,1)}, f32[32,128]{1,0:T(8,128)}) custom-call(bf16[88,8,32,128]{3,2,1,0:T(8,128)(2,1)} %basis_ref.1, bf16[88,8,32,128]{3,2,1,0:T(8,128)(2,1)} %image_ref.1, s32[8,32,128]{2,1,0:T(8,128)} %material_ref.1, s32[1,32]{1,0:T(1,128)} %bitcast.1), custom_call_target="tpu_custom_call" | custom-call | tf_op jit(solution)/shard_map/recycle_update/pallas_call | solution.py:469
  52.1 7.5 %times_inverse.1 = (f32[32,8,32,128]{3,2,1,0:T(8,128)}, f32[32,8,32,128]{3,2,1,0:T(8,128)}) custom-call(f32[32,128]{1,0:T(8,128)} %get-tuple-element.5.inverse_ref, bf16[8,32,64,128]{3,2,1,0:T(8,128)(2,1)} %get-tuple-element.6.rec_ref, bf16[8,32,64,128]{3,2,1,0:T(8,128)(2,1)} %get-tuple-element.7.app_ref), custom_call_target="tpu_custom_call" | custom-call | tf_op jit(solution)/shard_map/times_inverse/pallas_call | solution.py:504
